TPU v7x, 256 devices: a whole 4x4x8 slice. The times are simulated.
256 devices in a mesh: va: 8 (over z_hi, y), vb: 4 (over z_lo), oj: 8 (over x, core).
Axes of the slice: x: 4, y: 4, z: 8 (z_hi: 2, z_lo: 4; z = z_hi * 4 + z_lo), core: 2. Of those that a mesh axis runs over, the one named last changes fastest.
Arguments:
- occ_slab: bfloat16 [3584, 2, 2048], P(('vb', 'oj'), None, 'va'), may hold values from -0.875 to 0.875
- pair_slab: bfloat16 [3584, 8, 2048], P(('va', 'oj'), None, 'vb'), may hold values from -0.875 to 0.875
- occ_energy: float32 [2], replicated, may hold values from -1.5 to -0.3
- pair_energy: float32 [8], P('oj'), may hold values from -1.5 to -0.3
- vir_energy: float32 [2048], replicated, may hold values from 0.2 to 3
Outputs:
- gamma_occ: float32 [3584, 2, 2048], P(('vb', 'oj'), None, 'va')
- gamma_pair: float32 [3584, 8, 2048], P('va', 'oj', 'vb')
All inputs are finite; a program needn't handle non-finite values.
Results may differ from a plain program's by a relative error of at most 0.002.
Values may be sent and summed in bfloat16 or wider, within the bound.
A program may use at most 128 MiB of HBM per device.

v0:
```python
import jax
import jax.numpy as jnp
from jax import lax
from jax.sharding import PartitionSpec as P


def per_device(occ_slab, pair_slab, occ_energy, pair_energy, vir_energy):
    occ_full = lax.all_gather(occ_slab, ("vb", "oj"), axis=0, tiled=True)
    collected = lax.all_gather(pair_slab, "va", axis=0, tiled=True)
    mingled = lax.all_to_all(collected, "oj", split_axis=1, concat_axis=0, tiled=True)
    va_count = lax.axis_size("va")
    oj_count = lax.axis_size("oj")
    shaped = mingled.reshape(oj_count, va_count, -1, mingled.shape[1], mingled.shape[2])
    pair_full = jnp.swapaxes(shaped, 0, 1).reshape(-1, mingled.shape[1], mingled.shape[2])
    width_a = occ_full.shape[2]
    width_b = pair_full.shape[2]
    energy_a = lax.dynamic_slice_in_dim(vir_energy, lax.axis_index("va") * width_a, width_a)
    energy_b = lax.dynamic_slice_in_dim(vir_energy, lax.axis_index("vb") * width_b, width_b)
    pair_ints = jnp.einsum("qia,qjb->ijab", occ_full, pair_full, preferred_element_type=jnp.float32)
    denominator = (
        occ_energy[:, None, None, None]
        + pair_energy[None, :, None, None]
        - energy_a[None, None, :, None]
        - energy_b[None, None, None, :]
    )
    amplitudes = (pair_ints / denominator).astype(jnp.bfloat16)
    gamma_occ = lax.psum_scatter(
        jnp.einsum("ijab,qjb->qia", amplitudes, pair_full, preferred_element_type=jnp.float32),
        ("vb", "oj"),
        scatter_dimension=0,
        tiled=True,
    )
    gamma_pair = lax.psum_scatter(
        jnp.einsum("ijab,qia->qjb", amplitudes, occ_full, preferred_element_type=jnp.float32),
        "va",
        scatter_dimension=0,
        tiled=True,
    )
    return (gamma_occ, gamma_pair)


def solution(mesh):
    placed = (P(("vb", "oj"), None, "va"), P(("va", "oj"), None, "vb"), P(), P("oj"), P())
    return jax.shard_map(
        per_device,
        mesh=mesh,
        in_specs=placed,
        out_specs=(P(("vb", "oj"), None, "va"), P("va", "oj", "vb")),
        check_vma=False,
    )
```

profile of v0, /device:TPU:1, one launch (start us, length us, event | category | flops | bytes accessed | tf_op | source)
XLA Modules:
  0.0 833.1 jit_solution(16251034097933430811)
XLA Ops:
  7.2 0.0 all-gather.3.cloned.1.call-start
  7.2 1.9 copy.25
  9.1 0.0 all-gather.3.cloned.1.call-update
  9.2 0.0 all-gather.5.cloned.1.call-start
  9.2 1.6 copy.27
  10.8 0.0 all-gather.5.cloned.1.call-update
  10.8 0.0 copy-start.1
  10.8 103.1 %all-gather.3.cloned.1.call-done = bf16[448,8,512]{2,0,1:T(8,128)(2,1)} async-done(((bf16[56,8,512]{2,0,1:T(8,128)(2,1)}), bf16[448,8,512]{2,0,1:T(8,128)(2,1)}) %all-gather.3.cloned.1.call-update) | async-done | bytes 3670032 | tf_op jit(solution)/shard_map/all_gather | solution.py:9
  113.9 5.5 all-to-all-start
  119.4 0.0 all-reduce.7.cloned.1.call-start
  120.1 0.8 dynamic_slice.6
  120.8 0.8 dynamic_slice.7
  121.6 0.0 copy-done.1
  121.6 0.1 broadcast_subtract_fusion
  121.7 55.0 %all-to-all-done = bf16[448,8,512]{2,0,1:T(8,128)(2,1)} async-done(((bf16[448,8,512]{2,0,1:T(8,128)(2,1)}), bf16[448,8,512]{2,0,1:T(8,128)(2,1)}, u32[]{:S(2)}, u32[]{:S(2)}) %all-to-all-start) | async-done | bytes 3670048 | tf_op jit(solution)/shard_map/all_to_all | solution.py:10
  176.7 4.2 copy.26
  180.9 11.5 %all-gather.5.cloned.1.call-done = bf16[3584,2,256]{2,0,1:T(8,128)(2,1)} async-done(((bf16[112,2,256]{2,0,1:T(8,128)(2,1)}), bf16[3584,2,256]{2,0,1:T(8,128)(2,1)}) %all-gather.5.cloned.1.call-update) | async-done | bytes 3670032 | tf_op jit(solution)/shard_map/all_gather | solution.py:8
  192.5 5.4 fusion.2
  197.9 5.1 convolution_bitcast_fusion
  203.0 16.6 %copy.31 = f32[3584,1,512]{2,1,0:T(1,128)} copy(f32[3584,1,512]{0,2,1:T(8,128)} %convolution_bitcast_fusion) | data formatting | bytes 14680064 | tf_op jit(solution)/shard_map/ijab,qia->qjb/dot_general | solution.py:34
  219.6 0.0 all-reduce.7.cloned.1.call-update
  219.7 0.0 all-reduce.5.cloned.1.call-start
  219.7 7.1 convolution_bitcast_fusion.1
  226.8 11.7 %copy.30 = f32[3584,2,256]{2,1,0:T(2,128)} copy(f32[3584,2,256]{0,2,1:T(8,128)} %convolution_bitcast_fusion.1) | data formatting | bytes 14680064 | tf_op jit(solution)/shard_map/ijab,qjb->qia/dot_general | solution.py:28
  238.6 0.0 all-reduce.5.cloned.1.call-update
  238.6 0.6 copy-done.3
  239.2 0.6 dynamic-slice.2
  239.8 0.6 dynamic-slice
  241.7 289.5 %all-reduce.7.cloned.1.call-done = f32[3584,1,512]{2,1,0:T(1,128)} async-done(((f32[3584,1,512]{2,1,0:T(1,128)}), f32[3584,1,512]{2,1,0:T(1,128)}) %all-reduce.7.cloned.1.call-update) | async-done | bytes 7340048
  531.2 2.7 constant_dynamic-slice_fusion
  533.9 291.0 %all-reduce.5.cloned.1.call-done = f32[3584,2,256]{2,1,0:T(2,128)} async-done(((f32[3584,2,256]{2,1,0:T(2,128)}), f32[3584,2,256]{2,1,0:T(2,128)}) %all-reduce.5.cloned.1.call-update) | async-done | bytes 7340048
  824.9 1.6 constant_dynamic-slice_fusion.1
  (6 shorter events, 0.0 us)
Async XLA Ops:
  7.2 106.8 %all-gather.3.cloned.1.call-start = ((), (), s32[]{:S(2)}) async-start(), calls=%async_computation.1 | async-start | bytes 4128768 | tf_op jit(solution)/shard_map/all_gather | solution.py:9
  9.2 183.3 %all-gather.5.cloned.1.call-start = ((), (), s32[]{:S(2)}) async-start(), calls=%async_computation.2 | async-start | bytes 3784704 | tf_op jit(solution)/shard_map/all_gather | solution.py:8
  10.8 110.8 %copy-start.1 = (f32[2]{0:T(128)S(1)}, f32[2]{0:T(128)}, u32[]{:S(2)}) copy-start(f32[2]{0:T(128)} %param.7) | copy-start | bytes 28
  113.9 62.8 %all-to-all-start = ((bf16[448,8,512]{2,0,1:T(8,128)(2,1)}), bf16[448,8,512]{2,0,1:T(8,128)(2,1)}, u32[]{:S(2)}, u32[]{:S(2)}) async-start(bf16[448,8,512]{2,0,1:T(8,128)(2,1)} %all-gather.3.cloned.1.call-done), calls=%async_computation | async-start | bytes 7340032 | tf_op jit(solution)/shard_map/all_to_all | solution.py:10
  119.4 411.8 %all-reduce.7.cloned.1.call-start = ((), (), s32[]{:S(2)}) async-start(), calls=%async_computation.4 | async-start | bytes 14680064
  192.5 5.4 copy-start
  219.7 605.3 %all-reduce.5.cloned.1.call-start = ((), (), s32[]{:S(2)}) async-start(), calls=%async_computation.3 | async-start | bytes 14680064
  238.6 0.7 copy-start.3
  238.6 1.3 copy-start.2
Sparse Core Ops, SparseCore 0:
  11.1 102.7 all-gather.2
  116.3 76.1 all-gather.4
  219.8 311.3 all-reduce.6
  533.7 291.1 all-reduce.4
where the time goes:
time: 834 us; the launch traced here: 833 us
  waiting for transfers between devices  750 us (90%)
  local copies, waits for them, and re-layouts  43.8 us (5%)
  matrix products  17.6 us (2%)
  between operations  15.7 us (2%)
    unnamed x6, waiting for transfers between devices  581 us
    all_gather x1, waiting for transfers between devices, per_device(): collected = lax.all_gather(pair_slab, 'va', axis=0, tiled=True)  103 us
    all_to_all x1, waiting for transfers between devices, per_device(): lax.all_to_all(collected, 'oj', split_axis=1, concat_axis=0, tiled=True)  55 us
  transfers between devices with their start and end apart: 5, of which 5 were waited for; matrix products, arithmetic and copies ran while one was open for 4% of the time, Pallas kernels for 0%

commit v1 on v0

--- a/solution.py
+++ b/solution.py
@@ -4,10 +4,26 @@
 from jax.sharding import PartitionSpec as P
 
 
+def pairwise_exchange(x, axis, split, join):
+    ways, here = (lax.axis_size(axis), lax.axis_index(axis))
+    width = x.shape[split] // ways
+    dims = list(x.shape)
+    dims[split] = width
+    height = dims[join]
+    dims[join] = height * ways
+    full = jnp.zeros(dims, x.dtype)
+    for mask in range(ways):
+        part = lax.dynamic_slice_in_dim(x, (here ^ mask) * width, width, axis=split)
+        if mask:
+            part = lax.ppermute(part, axis, [(d, d ^ mask) for d in range(ways)])
+        full = lax.dynamic_update_slice_in_dim(full, part, (here ^ mask) * height, axis=join)
+    return full
+
+
 def per_device(occ_slab, pair_slab, occ_energy, pair_energy, vir_energy):
     occ_full = lax.all_gather(occ_slab, ("vb", "oj"), axis=0, tiled=True)
     collected = lax.all_gather(pair_slab, "va", axis=0, tiled=True)
-    mingled = lax.all_to_all(collected, "oj", split_axis=1, concat_axis=0, tiled=True)
+    mingled = pairwise_exchange(collected, "oj", 1, 0)
     va_count = lax.axis_size("va")
     oj_count = lax.axis_size("oj")
     shaped = mingled.reshape(oj_count, va_count, -1, mingled.shape[1], mingled.shape[2])

time: 834 us -> 700 us (0.84)
  waiting for transfers between devices: 750 us -> 602 us
    unnamed x6 -> x5, waiting for transfers between devices: 581 us -> 302 us
    reduce_scatter x0 -> x1, waiting for transfers between devices: none -> 144 us  [per_device(): lax.psum_scatter(jnp.einsum('ijab,qjb->qia', amplitudes, pair_full, prefe...]
    all_to_all x1 -> x0, waiting for transfers between devices: 55 us -> none  [per_device(): lax.all_to_all(collected, 'oj', split_axis=1, concat_axis=0, tiled=True)]
    ppermute x0 -> x7, waiting for transfers between devices: none -> 34.4 us  [pairwise_exchange(): part = lax.ppermute(part, axis, [(d, d ^ mask) for d in range(ways)])]
    ppermute x0 -> x7, starting transfers between devices: none -> 13.4 us  [pairwise_exchange(): part = lax.ppermute(part, axis, [(d, d ^ mask) for d in range(ways)])]
    dot_general x1 -> x0, local copies, waits for them, and re-layouts: 11.7 us -> none  [per_device(): jnp.einsum('ijab,qjb->qia', amplitudes, pair_full, preferred_element_type...]
    dynamic_update_slice x0 -> x7, local copies, waits for them, and re-layouts: none -> 9.85 us  [pairwise_exchange(): lax.dynamic_update_slice_in_dim(full, part, (here ^ mask) * height, axis=...]
  transfers between devices with their start and end apart: 5 -> 11, of which waited for: 5 -> 8; matrix products, arithmetic and copies ran while one was open for 4% -> 4% of each run, Pallas kernels for 0% -> 0%
where the time goes in v1:
time: 700 us; the launch traced here: 694 us
  waiting for transfers between devices  602 us (86%)
  local copies, waits for them, and re-layouts  46 us (7%)
  matrix products  17.6 us (3%)
  between operations  15.2 us (2%)
  starting transfers between devices  13.6 us (2%)
    unnamed x5, waiting for transfers between devices  302 us
    reduce_scatter x1, waiting for transfers between devices, per_device(): lax.psum_scatter(jnp.einsum('ijab,qjb->qia', amplitudes, pair_full, prefe...  144 us
    all_gather x1, waiting for transfers between devices, per_device(): collected = lax.all_gather(pair_slab, 'va', axis=0, tiled=True)  103 us
    ppermute x7, waiting for transfers between devices, pairwise_exchange(): part = lax.ppermute(part, axis, [(d, d ^ mask) for d in range(ways)])  34.4 us
    all_gather x1, waiting for transfers between devices, per_device(): occ_full = lax.all_gather(occ_slab, ('vb', 'oj'), axis=0, tiled=True)  18.3 us
    dot_general x1, local copies, waits for them, and re-layouts, per_device(): jnp.einsum('ijab,qia->qjb', amplitudes, occ_full, preferred_element_type=...  16.7 us
  transfers between devices with their start and end apart: 11, of which 8 were waited for; matrix products, arithmetic and copies ran while one was open for 4% of the time, Pallas kernels for 0%

profile of v1, /device:TPU:1, one launch (start us, length us, event | category | flops | bytes accessed | tf_op | source)
XLA Modules:
  0.0 694.4 jit_solution(7591994752999357186)
XLA Ops:
  7.2 1.9 copy.25
  9.2 1.6 copy.27
  10.9 103.1 %all-gather.3.cloned.1.call-done = bf16[448,8,512]{2,0,1:T(8,128)(2,1)} async-done(((bf16[56,8,512]{2,0,1:T(8,128)(2,1)}), bf16[448,8,512]{2,0,1:T(8,128)(2,1)}) %all-gather.3.cloned.1.call-update) | async-done | bytes 3670032 | tf_op jit(solution)/shard_map/all_gather | solution.py:25
  113.9 2.2 broadcast_in_dim.2
  116.1 1.2 copy-done
  117.3 1.1 constant_dynamic-slice_fusion
  118.4 1.1 collective-permute-start
  120.1 1.3 collective-permute-start.1
  122.6 2.7 collective-permute-start.3
  126.8 2.4 collective-permute-start.5
  129.2 1.8 constant_dynamic-update-slice_fusion.6
  131.1 5.6 collective-permute-done.1
  136.6 4.9 collective-permute-start.6
  141.5 1.9 constant_dynamic-update-slice_fusion.5
  143.4 10.2 %collective-permute-done.2 = bf16[448,1,512]{2,0,1:T(8,128)(2,1)} collective-permute-done((bf16[448,1,512]{2,0,1:T(8,128)(2,1)S(1)}, bf16[448,1,512]{2,0,1:T(8,128)(2,1)}, u32[]{:S(2)}, u32[]{:S(2)}) %collective-permute-start.2) | collective-permute-done | bytes 458784 | tf_op jit(solution)/shard_map/ppermute | solution.py:18
  153.6 1.9 constant_dynamic-update-slice_fusion.4
  155.4 10.5 %collective-permute-done.3 = bf16[448,1,512]{2,0,1:T(8,128)(2,1)} collective-permute-done((bf16[448,1,512]{2,0,1:T(8,128)(2,1)S(1)}, bf16[448,1,512]{2,0,1:T(8,128)(2,1)}, u32[]{:S(2)}, u32[]{:S(2)}) %collective-permute-start.3) | collective-permute-done | bytes 458784 | tf_op jit(solution)/shard_map/ppermute | solution.py:18
  165.9 1.8 constant_dynamic-update-slice_fusion.3
  167.7 8.2 %collective-permute-done.4 = bf16[448,1,512]{2,0,1:T(8,128)(2,1)S(1)} collective-permute-done((bf16[448,1,512]{2,0,1:T(8,128)(2,1)S(1)}, bf16[448,1,512]{2,0,1:T(8,128)(2,1)S(1)}, u32[]{:S(2)}, u32[]{:S(2)}) %collective-permute-start.4) | collective-permute-done | bytes 458784 | tf_op jit(solution)/shard_map/ppermute | solution.py:18
  175.9 0.8 constant_dynamic-update-slice_fusion.2
  176.7 0.8 constant_dynamic-update-slice_fusion.1
  177.5 0.8 constant_dynamic-update-slice_fusion
  178.4 4.3 copy.26
  182.7 18.3 %all-gather.5.cloned.1.call-done = bf16[3584,2,256]{2,0,1:T(8,128)(2,1)} async-done(((bf16[112,2,256]{2,0,1:T(8,128)(2,1)}), bf16[3584,2,256]{2,0,1:T(8,128)(2,1)}) %all-gather.5.cloned.1.call-update) | async-done | bytes 3670032 | tf_op jit(solution)/shard_map/all_gather | solution.py:24
  201.0 5.4 fusion.2
  206.4 5.1 convolution_bitcast_fusion
  211.5 16.7 %copy.30 = f32[3584,1,512]{2,1,0:T(1,128)} copy(f32[3584,1,512]{0,2,1:T(8,128)} %convolution_bitcast_fusion) | data formatting | bytes 14680064 | tf_op jit(solution)/shard_map/ijab,qia->qjb/dot_general | solution.py:50
  228.3 7.0 %fusion.3 = f32[3584,2,256]{2,0,1:T(8,128)} fusion(bf16[3584,512,1]{1,0,2:T(8,128)(2,1)} %bitcast.35, bf16[2,256,512]{1,2,0:T(8,128)(2,1)S(1)} %fusion.2), kind=kOutput, calls=%fused_computation.23 | convolution fusion | flops 1879048192 | bytes 11534336 | tf_op jit(solution)/shard_map/ijab,qjb->qia/dot_general | solution.py:44
  237.2 302.4 %all-reduce.3.cloned.1.call-done = f32[3584,1,512]{2,1,0:T(1,128)} async-done(((f32[3584,1,512]{2,1,0:T(1,128)}), f32[3584,1,512]{2,1,0:T(1,128)}) %all-reduce.3.cloned.1.call-update) | async-done | bytes 7340048
  539.6 2.7 constant_dynamic-slice_fusion.7
  542.3 143.8 %reduce-scatter.2.cloned.1.call-done = f32[112,2,256]{2,0,1:T(8,128)} async-done(((f32[3584,2,256]{2,0,1:T(8,128)}), f32[112,2,256]{2,0,1:T(8,128)}) %reduce-scatter.2.cloned.1.call-update) | async-done | bytes 229392 | tf_op jit(solution)/shard_map/reduce_scatter | solution.py:43
  686.1 1.8 copy.31
  (25 shorter events, 4.2 us)
Async XLA Ops:
  7.2 106.8 %all-gather.3.cloned.1.call-start = ((), (), s32[]{:S(2)}) async-start(), calls=%async_computation.1 | async-start | bytes 4128768 | tf_op jit(solution)/shard_map/all_gather | solution.py:25
  9.2 191.8 %all-gather.5.cloned.1.call-start = ((), (), s32[]{:S(2)}) async-start(), calls=%async_computation.2 | async-start | bytes 3784704 | tf_op jit(solution)/shard_map/all_gather | solution.py:24
  10.8 528.8 %all-reduce.3.cloned.1.call-start = ((), (), s32[]{:S(2)}) async-start(), calls=%async_computation.4 | async-start | bytes 14680064
  113.9 3.4 copy-start
  117.3 4.1 copy-start.2
  118.4 8.4 %collective-permute-start = (bf16[448,1,512]{2,0,1:T(8,128)(2,1)S(1)}, bf16[448,1,512]{2,0,1:T(8,128)(2,1)}, u32[]{:S(2)}, u32[]{:S(2)}) collective-permute-start(bf16[448,1,512]{2,0,1:T(8,128)(2,1)S(1)} %get-tuple-element.16), channel_id=1, source_target_pairs={{0,1},{1,0},{2,3},{3,2},{4,5},{5,4},{6,7},{7,6},{8,9},{9,8},{10,11... | collective-permute-start | bytes 1376264 | tf_op jit(solution)/shard_map/ppermute | solution.py:18
  120.1 16.6 %collective-permute-start.1 = (bf16[448,1,512]{2,0,1:T(8,128)(2,1)S(1)}, bf16[448,1,512]{2,0,1:T(8,128)(2,1)}, u32[]{:S(2)}, u32[]{:S(2)}) collective-permute-start(bf16[448,1,512]{2,0,1:T(8,128)(2,1)S(1)} %get-tuple-element.15), channel_id=1, source_target_pairs={{0,2},{1,3},{2,0},{3,1},{4,6},{5,7},{6,4},{7,5},{8,10},{9,11},{10,... | collective-permute-start | bytes 1376264 | tf_op jit(solution)/shard_map/ppermute | solution.py:18
  122.1 31.4 %collective-permute-start.2 = (bf16[448,1,512]{2,0,1:T(8,128)(2,1)S(1)}, bf16[448,1,512]{2,0,1:T(8,128)(2,1)}, u32[]{:S(2)}, u32[]{:S(2)}) collective-permute-start(bf16[448,1,512]{2,0,1:T(8,128)(2,1)S(1)} %get-tuple-element.14), channel_id=1, source_target_pairs={{0,3},{1,2},{2,1},{3,0},{4,7},{5,6},{6,5},{7,4},{8,11},{9,10},{10,... | collective-permute-start | bytes 1376264 | tf_op jit(solution)/shard_map/ppermute | solution.py:18
  122.6 43.3 %collective-permute-start.3 = (bf16[448,1,512]{2,0,1:T(8,128)(2,1)S(1)}, bf16[448,1,512]{2,0,1:T(8,128)(2,1)}, u32[]{:S(2)}, u32[]{:S(2)}) collective-permute-start(bf16[448,1,512]{2,0,1:T(8,128)(2,1)S(1)} %get-tuple-element.13), channel_id=1, source_target_pairs={{0,4},{1,5},{2,6},{3,7},{4,0},{5,1},{6,2},{7,3},{8,12},{9,13},{10,... | collective-permute-start | bytes 1376264 | tf_op jit(solution)/shard_map/ppermute | solution.py:18
  126.1 49.8 %collective-permute-start.4 = (bf16[448,1,512]{2,0,1:T(8,128)(2,1)S(1)}, bf16[448,1,512]{2,0,1:T(8,128)(2,1)S(1)}, u32[]{:S(2)}, u32[]{:S(2)}) collective-permute-start(bf16[448,1,512]{2,0,1:T(8,128)(2,1)S(1)} %get-tuple-element.12), channel_id=1, source_target_pairs={{0,5},{1,4},{2,7},{3,6},{4,1},{5,0},{6,3},{7,2},{8,13},{9,12},{10,... | collective-permute-start | bytes 1376264 | tf_op jit(solution)/shard_map/ppermute | solution.py:18
  126.8 49.9 %collective-permute-start.5 = (bf16[448,1,512]{2,0,1:T(8,128)(2,1)S(1)}, bf16[448,1,512]{2,0,1:T(8,128)(2,1)S(1)}, u32[]{:S(2)}, u32[]{:S(2)}) collective-permute-start(bf16[448,1,512]{2,0,1:T(8,128)(2,1)S(1)} %get-tuple-element.11), channel_id=1, source_target_pairs={{0,6},{1,7},{2,4},{3,5},{4,2},{5,3},{6,0},{7,1},{8,14},{9,15},{10,... | collective-permute-start | bytes 1376264 | tf_op jit(solution)/shard_map/ppermute | solution.py:18
  136.6 40.9 %collective-permute-start.6 = (bf16[448,1,512]{2,0,1:T(8,128)(2,1)S(1)}, bf16[448,1,512]{2,0,1:T(8,128)(2,1)S(1)}, u32[]{:S(2)}, u32[]{:S(2)}) collective-permute-start(bf16[448,1,512]{2,0,1:T(8,128)(2,1)S(1)} %get-tuple-element.10), channel_id=1, source_target_pairs={{0,7},{1,6},{2,5},{3,4},{4,3},{5,2},{6,1},{7,0},{8,15},{9,14},{10,... | collective-permute-start | bytes 1376264 | tf_op jit(solution)/shard_map/ppermute | solution.py:18
  201.0 5.4 copy-start.1
  228.2 457.9 %reduce-scatter.2.cloned.1.call-start = ((), (), s32[]{:S(2)}) async-start(), calls=%async_computation.3 | async-start | bytes 7569408 | tf_op jit(solution)/shard_map/reduce_scatter | solution.py:43
  235.3 0.7 copy-start.3
Sparse Core Ops, SparseCore 0:
  11.1 102.7 all-gather.2
  116.3 84.6 all-gather.4
  228.3 311.2 all-reduce.2
  542.0 144.0 reduce-scatter.1
